TPU v7x, 32 devices: a whole 2x2x4 slice. The times are simulated.
32 devices in a mesh: seq: 4 (over z), dp: 8 (over y, x, core).
Axes of the slice: x: 2, y: 2, z: 4, core: 2. Of those that a mesh axis runs over, the one named last changes fastest.
Arguments:
- tokens: bfloat16 [8, 1024, 768], P('dp', 'seq'), may hold values from -6 to 6
- qkv_weight: bfloat16 [768, 2304], P('dp'), may hold values from -0.21875 to 0.21875
- proj_weight: bfloat16 [768, 768], P('dp'), may hold values from -0.875 to 0.875
- hidden_weight: bfloat16 [768, 3072], P('dp'), may hold values from -0.21875 to 0.21875
- output_weight: bfloat16 [3072, 768], P('dp'), may hold values from -0.109375 to 0.109375
- first_gain: bfloat16 [768], P('dp'), may hold values from 0.25 to 1.75
- first_bias: bfloat16 [768], P('dp'), may hold values from -2.5 to 2.5
- second_gain: bfloat16 [768], P('dp'), may hold values from 0.25 to 1.75
- second_bias: bfloat16 [768], P('dp'), may hold values from -2.5 to 2.5
- cotangent: bfloat16 [8, 1024, 768], P('dp', 'seq'), may hold values from -6 to 6
Outputs:
- block_out: bfloat16 [8, 1024, 768], P('dp', 'seq')
- tokens_gradient: bfloat16 [8, 1024, 768], P('dp', 'seq')
- qkv_gradient: float32 [768, 2304], P('dp')
- proj_gradient: float32 [768, 768], P('dp')
- hidden_gradient: float32 [768, 3072], P('dp')
- output_gradient: float32 [3072, 768], P('dp')
- first_gain_gradient: float32 [768], P('dp')
- first_bias_gradient: float32 [768], P('dp')
- second_gain_gradient: float32 [768], P('dp')
- second_bias_gradient: float32 [768], P('dp')
All inputs are finite; a program needn't handle non-finite values.
Results may differ from a plain program's by a relative error of at most 0.012.
Values may be sent and summed in bfloat16 or wider, within the bound.
A program may use at most 256 MiB of HBM per device.

v0:
```python
import jax
import jax.numpy as jnp
from jax import lax
from jax.sharding import PartitionSpec as P

HEAD_DIM = 64
LOW = jnp.bfloat16
F32 = jnp.float32


def layer_norm(values, gain, bias):
    average = jnp.mean(values, -1, keepdims=True)
    centred = values - average
    variance = jnp.mean(centred * centred, -1, keepdims=True)
    return centred * lax.rsqrt(variance + 1e-05) * gain + bias


def gelu_tanh(values):
    return jax.nn.gelu(values, approximate=True)


def matmul(left, right):
    return jnp.dot(left, right, preferred_element_type=F32)


def matmul_left_t(left, right):
    return lax.dot_general(left, right, (((0,), (0,)), ((), ())), preferred_element_type=F32)


def matmul_right_t(left, right):
    return lax.dot_general(left, right, (((1,), (1,)), ((), ())), preferred_element_type=F32)


def gather_seq(value):
    return lax.all_gather(value, "seq", axis=0, tiled=True)


def scatter_seq(value):
    return lax.psum_scatter(value.astype(LOW), "seq", scatter_dimension=0, tiled=True).astype(F32)


def attention_forward(queries, keys, values):
    length, local_width = queries.shape
    heads_here = local_width // HEAD_DIM
    block_rows = min(512, length)
    blocks = length // block_rows
    scale = HEAD_DIM ** (-0.5)
    outs, logs = ([], [])
    key_index = jnp.arange(length)
    for b in range(blocks):
        seen = (b + 1) * block_rows
        q = queries[b * block_rows : seen].reshape(block_rows, heads_here, HEAD_DIM)
        k = keys[:seen].reshape(seen, heads_here, HEAD_DIM)
        v = values[:seen].reshape(seen, heads_here, HEAD_DIM)
        raw = jnp.einsum("qhd,khd->hqk", q, k, preferred_element_type=F32)
        positions = b * block_rows + jnp.arange(block_rows)
        causal = key_index[None, :seen] <= positions[:, None]
        scores = jnp.where(causal[None], raw * scale, -1e30)
        largest = jnp.max(scores, -1, keepdims=True)
        expo = jnp.exp(scores - largest)
        total = jnp.sum(expo, -1, keepdims=True)
        probs = (expo / total).astype(LOW)
        context = jnp.einsum("hqk,khd->qhd", probs, v, preferred_element_type=F32)
        outs.append(context.astype(LOW).reshape(block_rows, local_width))
        logs.append(largest + jnp.log(total))
    return (jnp.concatenate(outs, axis=0), logs)


def attention_backward(queries, keys, values, grads, logs):
    length, local_width = queries.shape
    heads_here = local_width // HEAD_DIM
    block_rows = min(512, length)
    blocks = length // block_rows
    scale = HEAD_DIM ** (-0.5)
    key_index = jnp.arange(length)
    query_grads = []
    key_sum = jnp.zeros((length, heads_here, HEAD_DIM), F32)
    value_sum = jnp.zeros((length, heads_here, HEAD_DIM), F32)
    for b in range(blocks):
        seen = (b + 1) * block_rows
        q = queries[b * block_rows : seen].reshape(block_rows, heads_here, HEAD_DIM)
        g = grads[b * block_rows : seen].reshape(block_rows, heads_here, HEAD_DIM)
        k = keys[:seen].reshape(seen, heads_here, HEAD_DIM)
        v = values[:seen].reshape(seen, heads_here, HEAD_DIM)
        raw = jnp.einsum("qhd,khd->hqk", q, k, preferred_element_type=F32)
        positions = b * block_rows + jnp.arange(block_rows)
        causal = key_index[None, :seen] <= positions[:, None]
        scores = jnp.where(causal[None], raw * scale, -1e30)
        probs = jnp.exp(scores - logs[b])
        low_probs = probs.astype(LOW)
        value_term = jnp.einsum("hqk,qhd->khd", low_probs, g, preferred_element_type=F32)
        prob_grad = jnp.einsum("qhd,khd->hqk", g, v, preferred_element_type=F32)
        score_grad = (probs * (prob_grad - jnp.sum(probs * prob_grad, -1, keepdims=True))).astype(
            LOW
        )
        query_grad = jnp.einsum("hqk,khd->qhd", score_grad, k, preferred_element_type=F32) * scale
        key_term = jnp.einsum("hqk,qhd->khd", score_grad, q, preferred_element_type=F32) * scale
        pad = ((0, length - seen), (0, 0), (0, 0))
        key_sum = key_sum + jnp.pad(key_term, pad)
        value_sum = value_sum + jnp.pad(value_term, pad)
        query_grads.append(query_grad.astype(LOW).reshape(block_rows, local_width))
    return (
        jnp.concatenate(query_grads, axis=0),
        key_sum.astype(LOW).reshape(length, local_width),
        value_sum.astype(LOW).reshape(length, local_width),
    )


def on_device(
    tokens,
    qkv_weight,
    proj_weight,
    hidden_weight,
    output_weight,
    first_gain,
    first_bias,
    second_gain,
    second_bias,
    cotangent,
):
    parts = lax.axis_size("seq")
    groups = lax.axis_size("dp")
    part = lax.axis_index("seq")
    inputs_low = tokens[0]
    rows, width = inputs_low.shape
    model_rows = qkv_weight.shape[0]
    local_width = width // parts
    hidden_rows = output_weight.shape[0] // parts
    hidden_here = hidden_rows * groups
    qkv_here = lax.dynamic_index_in_dim(
        qkv_weight.reshape(model_rows, 3, parts, local_width), part, 2, keepdims=False
    ).reshape(model_rows, 3 * local_width)
    hidden_cols = lax.dynamic_index_in_dim(
        hidden_weight.reshape(model_rows, groups, parts, hidden_rows), part, 2, keepdims=False
    ).reshape(model_rows, hidden_here)
    output_here = lax.dynamic_slice_in_dim(output_weight, part * hidden_rows, hidden_rows, 0)
    norms = jnp.stack([first_gain, first_bias, second_gain, second_bias], axis=0)
    norms = lax.all_gather(norms, "dp", axis=1, tiled=True).astype(F32)
    gain_one, bias_one, gain_two, bias_two = (norms[0], norms[1], norms[2], norms[3])
    all_tokens = gather_seq(inputs_low)
    wide_qkv = lax.all_gather(qkv_here, "dp", axis=0, tiled=True)
    wide_proj = lax.all_gather(proj_weight, "dp", axis=0, tiled=True)
    wide_hidden = lax.all_gather(hidden_cols, "dp", axis=0, tiled=True)
    wide_output = lax.all_gather(output_here, "dp", axis=0, tiled=True)
    all_grads = gather_seq(cotangent[0])
    inputs = all_tokens.astype(F32)
    lowered_one = layer_norm(inputs, gain_one, bias_one).astype(LOW)
    projected = matmul(lowered_one, wide_qkv).astype(LOW)
    queries = projected[:, :local_width]
    keys = projected[:, local_width : 2 * local_width]
    values = projected[:, 2 * local_width :]
    context_here, logs = attention_forward(queries, keys, values)
    context = lax.all_gather(context_here, "seq", axis=1, tiled=True)
    middle = inputs + matmul(context, wide_proj)
    lowered_two = layer_norm(middle, gain_two, bias_two).astype(LOW)
    hidden_pre = matmul(lowered_two, wide_hidden)
    activated_float, gelu_pull = jax.vjp(gelu_tanh, hidden_pre)
    activated = activated_float.astype(LOW)
    act_grad = matmul_right_t(all_grads, wide_output)
    pre_grad = gelu_pull(act_grad)[0].astype(LOW)
    normed_two_grad = scatter_seq(matmul_right_t(pre_grad, wide_hidden))
    ffn_out = scatter_seq(matmul(activated, wide_output))
    middle_own = lax.dynamic_slice_in_dim(middle, part * rows, rows, 0)
    block_out = middle_own + ffn_out
    _, norm_pull_two = jax.vjp(layer_norm, middle_own, gain_two, bias_two)
    middle_part, gain_two_term, bias_two_term = norm_pull_two(normed_two_grad)
    middle_grad = cotangent[0].astype(F32) + middle_part
    attn_grad = gather_seq(middle_grad.astype(LOW))
    proj_here = lax.dynamic_slice_in_dim(wide_proj, part * local_width, local_width, 0)
    context_grad = matmul_right_t(attn_grad, proj_here).astype(LOW)
    query_grads, key_grads, value_grads = attention_backward(
        queries, keys, values, context_grad, logs
    )
    qkv_grad = jnp.concatenate([query_grads, key_grads, value_grads], axis=1)
    normed_one_grad = scatter_seq(matmul_right_t(qkv_grad, wide_qkv))
    _, norm_pull_one = jax.vjp(layer_norm, inputs_low.astype(F32), gain_one, bias_one)
    input_part, gain_one_term, bias_one_term = norm_pull_one(normed_one_grad)
    tokens_gradient = (middle_grad + input_part).astype(LOW)
    attn_cols = lax.dynamic_slice_in_dim(attn_grad, part * local_width, local_width, 1)
    output_term = matmul_left_t(activated, all_grads).astype(LOW)
    hidden_term = matmul_left_t(lowered_two, pre_grad).astype(LOW)
    proj_term = matmul_left_t(context, attn_cols).astype(LOW)
    qkv_term = matmul_left_t(lowered_one, qkv_grad).astype(LOW)
    first_terms = jnp.concatenate([output_term, hidden_term], axis=1)
    second_terms = jnp.concatenate([proj_term, qkv_term], axis=1)
    first_sum = lax.psum_scatter(first_terms, "dp", scatter_dimension=0, tiled=True)
    second_sum = lax.psum_scatter(second_terms, "dp", scatter_dimension=0, tiled=True)
    first_all = lax.all_gather(first_sum, "seq", axis=0)
    second_all = lax.all_gather(second_sum, "seq", axis=0)
    output_gradient = first_all[:, :, :width].reshape(parts * hidden_rows, width).astype(F32)
    hidden_gradient = (
        first_all[:, :, width:]
        .reshape(parts, model_rows, groups, hidden_rows)
        .transpose(1, 2, 0, 3)
        .reshape(model_rows, parts * hidden_here)
        .astype(F32)
    )
    proj_gradient = (
        second_all[:, :, :local_width].transpose(1, 0, 2).reshape(model_rows, width).astype(F32)
    )
    qkv_gradient = (
        second_all[:, :, local_width:]
        .reshape(parts, model_rows, 3, local_width)
        .transpose(1, 2, 0, 3)
        .reshape(model_rows, 3 * width)
        .astype(F32)
    )
    norm_terms = jnp.stack([gain_one_term, bias_one_term, gain_two_term, bias_two_term], axis=0)
    norm_sum = lax.psum(norm_terms, ("seq", "dp"))
    norm_own = lax.dynamic_slice_in_dim(
        norm_sum, lax.axis_index("dp") * first_gain.shape[0], first_gain.shape[0], 1
    )
    return (
        block_out.astype(LOW)[None],
        tokens_gradient[None],
        qkv_gradient,
        proj_gradient,
        hidden_gradient,
        output_gradient,
        norm_own[0],
        norm_own[1],
        norm_own[2],
        norm_own[3],
    )


def solution(mesh):
    placed = (
        P("dp", "seq", None),
        P("dp", None),
        P("dp", None),
        P("dp", None),
        P("dp", None),
        P("dp"),
        P("dp"),
        P("dp"),
        P("dp"),
        P("dp", "seq", None),
    )
    return jax.shard_map(
        on_device,
        mesh=mesh,
        in_specs=placed,
        out_specs=(
            P("dp", "seq", None),
            P("dp", "seq", None),
            P("dp", None),
            P("dp", None),
            P("dp", None),
            P("dp", None),
            P("dp"),
            P("dp"),
            P("dp"),
            P("dp"),
        ),
        check_vma=False,
    )
```

profile of v0, /device:TPU:0, one launch (start us, length us, event | category | flops | bytes accessed | tf_op | source)
XLA Modules:
  0.0 499.9 jit_solution(855848961846258834)
XLA Ops:
  7.2 2.0 copy.123
  10.8 10.3 %all-gather.4 = bf16[8,96,4]{1,2,0:T(4,128)(2,1)S(1)} all-gather(bf16[1,96,4]{1,2,0:T(4,128)(2,1)S(1)} %maximum_bitcast_fusion), channel_id=1, replica_groups=mesh['seq'=4,'dp'=8] {'dp'}, dimensions={0}, use_global_device_ids=true | all-gather | bytes 6912 | tf_op jit(solution)/shard_map/all_gather | solution.py:138
  22.4 1.6 reshape.258
  24.7 11.9 %all_gather.41 = bf16[768,576]{1,0:T(8,128)(2,1)} all-gather(bf16[96,576]{1,0:T(8,128)(2,1)S(1)} %copy.126), channel_id=1, replica_groups=mesh['seq'=4,'dp'=8] {'dp'}, dimensions={0}, use_global_device_ids=true | all-gather | bytes 995328 | tf_op jit(solution)/shard_map/all_gather | solution.py:141
  36.7 13.9 %all-gather.24.cloned.1.call-done = bf16[1,1024,768]{1,2,0:T(8,128)(2,1)} async-done(((bf16[1,256,768]{1,2,0:T(8,128)(2,1)}), bf16[1,1024,768]{1,2,0:T(8,128)(2,1)}) %all-gather.24.cloned.1.call-update) | async-done | bytes 1572880 | tf_op jit(solution)/shard_map/all_gather | solution.py:35
  50.6 1.8 convert_reduce_fusion
  52.5 1.9 fusion.6
  59.2 1.5 fusion
  61.7 1.7 fusion.55
  69.1 5.8 %all-gather.16.cloned.1.call-done = bf16[768,768]{1,0:T(8,128)(2,1)} async-done(((bf16[96,768]{1,0:T(8,128)(2,1)}), bf16[768,768]{1,0:T(8,128)(2,1)}) %all-gather.16.cloned.1.call-update) | async-done | bytes 1179664 | tf_op jit(solution)/shard_map/all_gather | solution.py:142
  74.8 39.3 %all-gather.14.cloned.1.call-done = bf16[1024,768]{0,1:T(8,128)(2,1)} async-done(((bf16[1024,192]{0,1:T(8,128)(2,1)}), bf16[1024,768]{0,1:T(8,128)(2,1)}) %all-gather.14.cloned.1.call-update) | async-done | bytes 1572880 | tf_op jit(solution)/shard_map/all_gather | solution.py:153
  114.1 3.7 fusion.90
  118.5 1.7 add_convert_fusion
  120.2 19.2 %all-gather.18.cloned.1.call-done = bf16[768,768]{1,0:T(8,128)(2,1)} async-done(((bf16[96,768]{1,0:T(8,128)(2,1)}), bf16[768,768]{1,0:T(8,128)(2,1)}) %all-gather.18.cloned.1.call-update) | async-done | bytes 1179664 | tf_op jit(solution)/shard_map/all_gather | solution.py:143
  139.4 4.8 fusion.91
  144.2 21.0 %all-gather.20.cloned.1.call-done = bf16[768,768]{1,0:T(8,128)(2,1)} async-done(((bf16[96,768]{1,0:T(8,128)(2,1)}), bf16[768,768]{1,0:T(8,128)(2,1)}) %all-gather.20.cloned.1.call-update) | async-done | bytes 1179664 | tf_op jit(solution)/shard_map/all_gather | solution.py:144
  165.2 38.5 %all-gather.26.cloned.1.call-done = bf16[1,1024,768]{2,1,0:T(8,128)(2,1)} async-done(((bf16[1,256,768]{2,1,0:T(8,128)(2,1)}), bf16[1,1024,768]{2,1,0:T(8,128)(2,1)}) %all-gather.26.cloned.1.call-update) | async-done | bytes 1572880 | tf_op jit(solution)/shard_map/all_gather | solution.py:35
  203.8 5.6 %fusion.16 = bf16[1024,768]{1,0:T(8,128)(2,1)S(1)} fusion(f32[1024,768]{1,0:T(8,128)} %fusion.91, bf16[768,768]{1,0:T(8,128)(2,1)} %all-gather.20.cloned.1.call-done, bf16[1,1024,768]{2,1,0:T(8,128)(2,1)} %all-gather.26.cloned.1.call-done), kind=kOutput, calls=%fused_computation.26 | convolution fusion | flops 1223688192 | bytes 7471104 | tf_op jit(solution)/shard_map/dot_general | solution.py:31
  210.5 2.6 convolution_convert_fusion.1
  213.4 3.5 convolution_convert_fusion.3
  216.9 1.7 fusion.33
  218.6 1.5 pad_maximum_fusion
  220.2 4.3 copy.156
  224.6 1.9 copy.130
  227.2 20.3 %reduce-scatter.12.cloned.1.call-done = bf16[256,768]{0,1:T(8,128)(2,1)} async-done(((bf16[1024,768]{0,1:T(8,128)(2,1)}), bf16[256,768]{0,1:T(8,128)(2,1)}) %reduce-scatter.12.cloned.1.call-update) | async-done | bytes 393232 | tf_op jit(solution)/shard_map/reduce_scatter | solution.py:39
  247.5 2.0 multiply_reduce_fusion.3
  249.5 2.1 fusion.67
  252.2 2.7 fusion.70
  257.0 35.3 %reduce-scatter.18.cloned.1.call-done = bf16[96,1536]{1,0:T(8,128)(2,1)} async-done(((bf16[768,1536]{1,0:T(8,128)(2,1)}), bf16[96,1536]{1,0:T(8,128)(2,1)}) %reduce-scatter.18.cloned.1.call-update) | async-done | bytes 294928 | tf_op jit(solution)/shard_map/reduce_scatter | solution.py:186
  292.4 39.9 %all-gather.22.cloned.1.call-done = bf16[1024,768]{0,1:T(8,128)(2,1)} async-done(((bf16[256,768]{0,1:T(8,128)(2,1)}), bf16[1024,768]{0,1:T(8,128)(2,1)}) %all-gather.22.cloned.1.call-update) | async-done | bytes 1572880 | tf_op jit(solution)/shard_map/all_gather | solution.py:35
  332.3 2.0 convolution_convert_fusion.6
  334.4 1.5 multiply_reduce_fusion.1
  339.3 1.9 multiply_reduce_fusion
  344.0 1.7 convolution_convert_fusion.7
  351.5 2.5 convolution_convert_fusion
  354.3 5.0 %convolution_convert_fusion.2 = bf16[1024,768]{0,1:T(8,128)(2,1)} fusion(bf16[768,768]{1,0:T(8,128)(2,1)} %all-gather.20.cloned.1.call-done, f32[1024,768]{1,0:T(8,128)} %fusion.91), kind=kOutput, calls=%fused_computation.50 | convolution fusion | flops 1215823872 | bytes 5898240 | tf_op jit(solution)/shard_map/dot_general | solution.py:23
  362.5 2.4 fusion.84
  364.9 1.9 reshape.285
  366.9 2.2 copy.143
  369.0 3.6 reshape.282
  373.8 28.3 %reduce-scatter.16.cloned.1.call-done = bf16[96,768]{1,0:T(8,128)(2,1)} async-done(((bf16[768,768]{1,0:T(8,128)(2,1)}), bf16[96,768]{1,0:T(8,128)(2,1)}) %reduce-scatter.16.cloned.1.call-update) | async-done | bytes 147472 | tf_op jit(solution)/shard_map/reduce_scatter | solution.py:187
  402.0 22.2 %all-gather.2 = bf16[384,768]{1,0:T(8,128)(2,1)S(1)} all-gather(bf16[96,768]{1,0:T(8,128)(2,1)} %reduce-scatter.16.cloned.1.call-done), channel_id=4, replica_groups=mesh['seq'=4,'dp'=8] {'seq'}, dimensions={0}, use_global_device_ids=true | all-gather | bytes 737280 | tf_op jit(solution)/shard_map/all_gather | solution.py:189
  426.2 1.5 copy.140
  427.8 2.9 reshape.280
  430.7 13.6 %reduce-scatter.14.cloned.1.call-done = bf16[256,768]{0,1:T(8,128)(2,1)} async-done(((bf16[1024,768]{0,1:T(8,128)(2,1)}), bf16[256,768]{0,1:T(8,128)(2,1)}) %reduce-scatter.14.cloned.1.call-update) | async-done | bytes 393232 | tf_op jit(solution)/shard_map/reduce_scatter | solution.py:39
  445.8 1.5 fusion.68
  447.3 41.4 %psum.7 = f32[4,768]{1,0:T(4,128)S(1)} all-reduce(f32[4,768]{1,0:T(4,128)S(1)} %pad_maximum_fusion.6), channel_id=1, replica_groups=mesh['seq'=4,'dp'=8] {'seq','dp'}, use_global_device_ids=true, to_apply=%region_27.28 | all-reduce | flops 3072 | bytes 24576 | tf_op jit(solution)/shard_map/psum | solution.py:209
  489.3 2.0 fusion.73
  (212 shorter events, 42.5 us)
Async XLA Ops:
  7.2 60.5 %copy-start = (bf16[384,768]{1,0:T(8,128)(2,1)S(1)}, bf16[384,768]{1,0:T(8,128)(2,1)}, u32[]{:S(2)}) copy-start(bf16[384,768]{1,0:T(8,128)(2,1)} %param.14) | copy-start | bytes 1769476
  7.2 43.4 %all-gather.24.cloned.1.call-start = ((), (), s32[]{:S(2)}) async-start(), calls=%async_computation.13 | async-start | bytes 1966080 | tf_op jit(solution)/shard_map/all_gather | solution.py:35
  9.2 65.6 %all-gather.16.cloned.1.call-start = ((), (), s32[]{:S(2)}) async-start(), calls=%async_computation.6 | async-start | bytes 1327104 | tf_op jit(solution)/shard_map/all_gather | solution.py:142
  10.0 104.1 %all-gather.14.cloned.1.call-start = ((), (), s32[]{:S(2)}) async-start(), calls=%async_computation.5 | async-start | bytes 1966080 | tf_op jit(solution)/shard_map/all_gather | solution.py:153
  21.8 32.5 %copy-start.47 = (f32[768]{0:T(1024)}, f32[768]{0:T(1024)S(1)}, u32[]{:S(2)}) copy-start(f32[768]{0:T(1024)S(1)} %get-tuple-element.82) | copy-start | bytes 9220
  50.6 4.3 copy-start.7
  50.6 4.3 copy-start.19
  52.4 3.8 copy-start.36
  56.3 2.3 copy-start.11
  56.4 4.3 copy-start.21
  56.4 5.2 %copy-start.17 = (bf16[1024,192]{0,1:T(8,128)(2,1)}, bf16[1024,192]{0,1:T(8,128)(2,1)S(1)}, u32[]{:S(2)}) copy-start(bf16[1024,192]{0,1:T(8,128)(2,1)S(1)} %get-tuple-element.93) | copy-start | bytes 1179652
  57.2 3.5 copy-start.3
  58.7 3.0 copy-start.2
  58.7 3.0 copy-start.29
  61.7 3.0 copy-start.23
  64.2 75.2 %all-gather.18.cloned.1.call-start = ((), (), s32[]{:S(2)}) async-start(), calls=%async_computation.7 | async-start | bytes 1327104 | tf_op jit(solution)/shard_map/all_gather | solution.py:143
  67.6 97.6 %all-gather.20.cloned.1.call-start = ((), (), s32[]{:S(2)}) async-start(), calls=%async_computation.8 | async-start | bytes 1327104 | tf_op jit(solution)/shard_map/all_gather | solution.py:144
  68.4 135.3 %all-gather.26.cloned.1.call-start = ((), (), s32[]{:S(2)}) async-start(), calls=%async_computation.14 | async-start | bytes 1966080 | tf_op jit(solution)/shard_map/all_gather | solution.py:35
  69.0 178.5 %reduce-scatter.12.cloned.1.call-start = ((), (), s32[]{:S(2)}) async-start(), calls=%async_computation.10 | async-start | bytes 1966080 | tf_op jit(solution)/shard_map/reduce_scatter | solution.py:39
  117.9 131.6 %copy-start.5 = (f32[1024,768]{0,1:T(8,128)}, f32[1024,768]{0,1:T(8,128)S(1)}, u32[]{:S(2)}) copy-start(f32[1024,768]{0,1:T(8,128)S(1)} %get-tuple-element.109) | copy-start | bytes 9437188
  203.8 6.8 %copy-start.53 = (bf16[768,768]{1,0:T(8,128)(2,1)S(1)}, bf16[768,768]{1,0:T(8,128)(2,1)}, u32[]{:S(2)}) copy-start(bf16[768,768]{1,0:T(8,128)(2,1)} %all-gather.18.cloned.1.call-done) | copy-start | bytes 3538948
  213.2 79.1 %reduce-scatter.18.cloned.1.call-start = ((), (), s32[]{:S(2)}) async-start(), calls=%async_computation.17 | async-start | bytes 2654208 | tf_op jit(solution)/shard_map/reduce_scatter | solution.py:186
  213.4 3.5 copy-start.52
  213.4 3.5 copy-start.54
  224.5 107.8 %all-gather.22.cloned.1.call-start = ((), (), s32[]{:S(2)}) async-start(), calls=%async_computation.11 | async-start | bytes 1966080 | tf_op jit(solution)/shard_map/all_gather | solution.py:35
  251.6 82.8 %copy-start.4 = (f32[3,512,512]{1,2,0:T(8,128)S(1)}, f32[3,512,512]{1,2,0:T(8,128)}, u32[]{:S(2)}) copy-start(f32[3,512,512]{1,2,0:T(8,128)} %copy-done.3) | copy-start | bytes 9437188
  254.9 107.6 %all-gather.28.cloned.1.call-start = ((), (), s32[]{:S(2)}) async-start(), calls=%async_computation.15 | async-start | bytes 1474560 | tf_op jit(solution)/shard_map/all_gather | solution.py:188
  292.3 109.7 %reduce-scatter.16.cloned.1.call-start = ((), (), s32[]{:S(2)}) async-start(), calls=%async_computation.16 | async-start | bytes 1327104 | tf_op jit(solution)/shard_map/reduce_scatter | solution.py:187
  335.9 2.4 slice-start
  335.9 3.1 slice-start.1
  337.4 10.9 %copy-start.26 = (bf16[3,64,512]{2,1,0:T(8,128)(2,1)}, bf16[3,64,512]{2,1,0:T(8,128)(2,1)S(1)}, u32[]{:S(2)}) copy-start(bf16[3,64,512]{2,1,0:T(8,128)(2,1)S(1)} %fusion.52) | copy-start | bytes 589828
  342.6 3.2 copy-start.12
  344.0 4.3 copy-start.24
  351.4 92.9 %reduce-scatter.14.cloned.1.call-start = ((), (), s32[]{:S(2)}) async-start(), calls=%async_computation.12 | async-start | bytes 1966080 | tf_op jit(solution)/shard_map/reduce_scatter | solution.py:39
  354.1 5.4 %copy-start.6 = (bf16[1,256,768]{1,2,0:T(8,128)(2,1)S(1)}, bf16[1,256,768]{1,2,0:T(8,128)(2,1)}, u32[]{:S(2)}) copy-start(bf16[1,256,768]{1,2,0:T(8,128)(2,1)} %copy.123) | copy-start | bytes 1179652
  354.1 6.0 %copy-start.34 = (f32[768]{0:T(1024)S(1)}, f32[768]{0:T(1024)}, u32[]{:S(2)}) copy-start(f32[768]{0:T(1024)} %get-tuple-element.79) | copy-start | bytes 9220
  354.1 6.6 %copy-start.35 = (f32[768]{0:T(1024)S(1)}, f32[768]{0:T(1024)}, u32[]{:S(2)}) copy-start(f32[768]{0:T(1024)} %get-tuple-element.70) | copy-start | bytes 9220
  354.1 135.2 %reduce-scatter.10.cloned.1.call-start = ((), (), s32[]{:S(2)}) async-start(), calls=%async_computation.9 | async-start | bytes 1966080 | tf_op jit(solution)/shard_map/reduce_scatter | solution.py:39
  426.1 18.2 %copy-start.38 = (f32[256]{0:T(256)S(1)}, f32[256]{0:T(256)}, u32[]{:S(2)}) copy-start(f32[256]{0:T(256)} %broadcast_multiply_fusion.2) | copy-start | bytes 3076
  426.1 21.1 %copy-start.43 = (f32[1,768]{1,0:T(1,128)S(1)}, f32[1,768]{1,0:T(1,128)}, u32[]{:S(2)}) copy-start(f32[1,768]{1,0:T(1,128)} %reshape.279) | copy-start | bytes 9220
  426.1 21.1 %copy-start.44 = (f32[1,768]{1,0:T(1,128)S(1)}, f32[1,768]{1,0:T(1,128)}, u32[]{:S(2)}) copy-start(f32[1,768]{1,0:T(1,128)} %reshape.278) | copy-start | bytes 9220
  426.2 63.1 %copy-start.9 = (bf16[256,768]{0,1:T(8,128)(2,1)S(1)}, bf16[256,768]{0,1:T(8,128)(2,1)}, u32[]{:S(2)}) copy-start(bf16[256,768]{0,1:T(8,128)(2,1)} %reduce-scatter.12.cloned.1.call-done) | copy-start | bytes 1179652
  426.2 63.1 %copy-start.10 = (bf16[1,256,768]{1,2,0:T(8,128)(2,1)S(1)}, bf16[1,256,768]{1,2,0:T(8,128)(2,1)}, u32[]{:S(2)}) copy-start(bf16[1,256,768]{1,2,0:T(8,128)(2,1)} %copy.130) | copy-start | bytes 1179652
  426.2 63.1 %copy-start.32 = (f32[256]{0:T(256)S(1)}, f32[256]{0:T(256)}, u32[]{:S(2)}) copy-start(f32[256]{0:T(256)} %broadcast_multiply_fusion.3) | copy-start | bytes 3076
  426.2 63.1 %copy-start.40 = (f32[256]{0:T(256)S(1)}, f32[256]{0:T(256)}, u32[]{:S(2)}) copy-start(f32[256]{0:T(256)} %copy-done.39) | copy-start | bytes 3076
  426.2 63.1 %copy-start.42 = (f32[256]{0:T(256)S(1)}, f32[256]{0:T(256)}, u32[]{:S(2)}) copy-start(f32[256]{0:T(256)} %copy-done.41) | copy-start | bytes 3076
  426.2 63.1 %copy-start.46 = (f32[256]{0:T(256)S(1)}, f32[256]{0:T(256)}, u32[]{:S(2)}) copy-start(f32[256]{0:T(256)} %copy-done.45) | copy-start | bytes 3076
  444.3 48.9 %copy-start.1 = (bf16[384,768]{1,0:T(8,128)(2,1)S(1)}, bf16[384,768]{1,0:T(8,128)(2,1)}, u32[]{:S(2)}) copy-start(bf16[384,768]{1,0:T(8,128)(2,1)} %param.14) | copy-start | bytes 1769476
  (23 other events, 35.3 us)
Sparse Core Ops, SparseCore 0:
  10.2 40.3 all-gather.23
  52.5 22.3 all-gather.15
  77.0 37.0 all-gather.13
  116.4 22.9 all-gather.17
  141.1 24.0 all-gather.19
  166.6 37.0 all-gather.25
  213.3 34.1 reduce-scatter.11
  250.8 41.4 reduce-scatter.17
  294.5 37.6 all-gather.21
  333.8 28.7 all-gather.27
  366.1 35.8 reduce-scatter.15
  404.2 40.0 reduce-scatter.13
  446.6 35.2 reduce-scatter.9
where the time goes:
time: 508 us; the launch traced here: 500 us
  waiting for transfers between devices  278 us (55%)
  blocking collectives  85.8 us (17%)
  matrix products  48.4 us (10%)
  local copies, waits for them, and re-layouts  38.9 us (8%)
  other arithmetic  32.6 us (6%)
  between operations  15.1 us (3%)
    all_gather x3, waiting for transfers between devices, gather_seq(): return lax.all_gather(value, 'seq', axis=0, tiled=True)  92.4 us
    psum x1, blocking collectives, on_device(): norm_sum = lax.psum(norm_terms, ('seq', 'dp'))  41.4 us
    all_gather x1, waiting for transfers between devices, on_device(): context = lax.all_gather(context_here, 'seq', axis=1, tiled=True)  39.3 us
    reduce_scatter x1, waiting for transfers between devices, on_device(): lax.psum_scatter(first_terms, 'dp', scatter_dimension=0, tiled=True)  35.3 us
    reduce_scatter x3, waiting for transfers between devices, scatter_seq(): lax.psum_scatter(value.astype(LOW), 'seq', scatter_dimension=0, tiled=True)  33.9 us
    reduce_scatter x1, waiting for transfers between devices, on_device(): lax.psum_scatter(second_terms, 'dp', scatter_dimension=0, tiled=True)  28.3 us
    all_gather x1, blocking collectives, on_device(): second_all = lax.all_gather(second_sum, 'seq', axis=0)  22.2 us
    all_gather x1, waiting for transfers between devices, on_device(): wide_output = lax.all_gather(output_here, 'dp', axis=0, tiled=True)  21 us
  transfers between devices with their start and end apart: 13, of which 12 were waited for; matrix products, arithmetic and copies ran while one was open for 20% of the time, Pallas kernels for 0%

commit v1 on v0

--- a/solution.py
+++ b/solution.py
@@ -150,7 +150,12 @@
     keys = projected[:, local_width : 2 * local_width]
     values = projected[:, 2 * local_width :]
     context_here, logs = attention_forward(queries, keys, values)
-    context = lax.all_gather(context_here, "seq", axis=1, tiled=True)
+    ring = [context_here]
+    for hop in range(3):
+        ring.append(lax.ppermute(ring[-1], "seq", [(dev, (dev + 1) % 4) for dev in range(4)]))
+    context = jnp.roll(
+        jnp.concatenate(ring[::-1], axis=1), (lax.axis_index("seq") + 1) * ring[0].shape[1], axis=1
+    )
     middle = inputs + matmul(context, wide_proj)
     lowered_two = layer_norm(middle, gain_two, bias_two).astype(LOW)
     hidden_pre = matmul(lowered_two, wide_hidden)

time: 508 us -> 467 us (0.919)
  waiting for transfers between devices: 278 us -> 222 us
  local copies, waits for them, and re-layouts: 38.9 us -> 51.4 us
    all_gather x1 -> x0, waiting for transfers between devices: 39.3 us -> none  [on_device(): context = lax.all_gather(context_here, 'seq', axis=1, tiled=True)]
    ppermute x0 -> x3, waiting for transfers between devices: none -> 30.5 us  [on_device(): lax.ppermute(ring[-1], 'seq', [(dev, (dev + 1) % 4) for dev in range(4)])]
    all_gather x1, waiting for transfers between devices: 19.2 us -> 0.01 us  [on_device(): wide_hidden = lax.all_gather(hidden_cols, 'dp', axis=0, tiled=True)]
    all_gather x1, waiting for transfers between devices: 21 us -> 4.46 us  [on_device(): wide_output = lax.all_gather(output_here, 'dp', axis=0, tiled=True)]
    unnamed x123 -> x147, local copies, waits for them, and re-layouts: 16.8 us -> 28.8 us
    all_gather x1, waiting for transfers between devices: 5.78 us -> 0.01 us  [on_device(): wide_proj = lax.all_gather(proj_weight, 'dp', axis=0, tiled=True)]
  transfers between devices with their start and end apart: 13 -> 15, of which waited for: 12 -> 12; matrix products, arithmetic and copies ran while one was open for 20% -> 25% of each run, Pallas kernels for 0% -> 0%
where the time goes in v1:
time: 467 us; the launch traced here: 462 us
  waiting for transfers between devices  222 us (48%)
  blocking collectives  85.2 us (18%)
  local copies, waits for them, and re-layouts  51.4 us (11%)
  matrix products  49 us (10%)
  other arithmetic  36.5 us (8%)
  between operations  15.7 us (3%)
    all_gather x3, waiting for transfers between devices, gather_seq(): return lax.all_gather(value, 'seq', axis=0, tiled=True)  87.7 us
    psum x1, blocking collectives, on_device(): norm_sum = lax.psum(norm_terms, ('seq', 'dp'))  41.2 us
    reduce_scatter x1, waiting for transfers between devices, on_device(): lax.psum_scatter(first_terms, 'dp', scatter_dimension=0, tiled=True)  35.1 us
    reduce_scatter x3, waiting for transfers between devices, scatter_seq(): lax.psum_scatter(value.astype(LOW), 'seq', scatter_dimension=0, tiled=True)  32.9 us
    ppermute x3, waiting for transfers between devices, on_device(): lax.ppermute(ring[-1], 'seq', [(dev, (dev + 1) % 4) for dev in range(4)])  30.5 us
    unnamed x147, local copies, waits for them, and re-layouts  28.8 us
    reduce_scatter x1, waiting for transfers between devices, on_device(): lax.psum_scatter(second_terms, 'dp', scatter_dimension=0, tiled=True)  28.1 us
    all_gather x1, blocking collectives, on_device(): second_all = lax.all_gather(second_sum, 'seq', axis=0)  22.1 us
  transfers between devices with their start and end apart: 15, of which 12 were waited for; matrix products, arithmetic and copies ran while one was open for 25% of the time, Pallas kernels for 0%

profile of v1, /device:TPU:0, one launch (start us, length us, event | category | flops | bytes accessed | tf_op | source)
XLA Modules:
  0.0 461.7 jit_solution(7443774533642441649)
XLA Ops:
  7.3 2.0 copy.123
  10.1 2.3 reshape.268
  15.4 10.3 %all-gather.4 = bf16[8,96,4]{1,2,0:T(4,128)(2,1)S(1)} all-gather(bf16[1,96,4]{1,2,0:T(4,128)(2,1)S(1)} %maximum_bitcast_fusion), channel_id=1, replica_groups=mesh['seq'=4,'dp'=8] {'dp'}, dimensions={0}, use_global_device_ids=true | all-gather | bytes 6912 | tf_op jit(solution)/shard_map/all_gather | solution.py:138
  29.8 11.6 %all_gather.38 = bf16[768,576]{1,0:T(8,128)(2,1)S(1)} all-gather(bf16[96,576]{1,0:T(8,128)(2,1)S(1)} %copy.126), channel_id=1, replica_groups=mesh['seq'=4,'dp'=8] {'dp'}, dimensions={0}, use_global_device_ids=true | all-gather | bytes 995328 | tf_op jit(solution)/shard_map/all_gather | solution.py:141
  41.4 9.3 %all-gather.21.cloned.1.call-done = bf16[1,1024,768]{1,2,0:T(8,128)(2,1)} async-done(((bf16[1,256,768]{1,2,0:T(8,128)(2,1)}), bf16[1,1024,768]{1,2,0:T(8,128)(2,1)}) %all-gather.21.cloned.1.call-update) | async-done | bytes 1572880 | tf_op jit(solution)/shard_map/all_gather | solution.py:35
  50.7 1.8 convert_reduce_fusion
  52.5 1.9 fusion.6
  66.3 10.4 %collective-permute-done = bf16[1024,192]{0,1:T(8,128)(2,1)S(1)} collective-permute-done((bf16[1024,192]{0,1:T(8,128)(2,1)S(1)}, bf16[1024,192]{0,1:T(8,128)(2,1)S(1)}, u32[]{:S(2)}, u32[]{:S(2)}) %collective-permute-start) | collective-permute-done | bytes 393248 | tf_op jit(solution)/shard_map/ppermute | solution.py:155
  77.5 10.5 %collective-permute-done.1 = bf16[1024,192]{0,1:T(8,128)(2,1)} collective-permute-done((bf16[1024,192]{0,1:T(8,128)(2,1)S(1)}, bf16[1024,192]{0,1:T(8,128)(2,1)}, u32[]{:S(2)}, u32[]{:S(2)}) %collective-permute-start.1) | collective-permute-done | bytes 393248 | tf_op jit(solution)/shard_map/ppermute | solution.py:155
  88.3 9.6 %collective-permute-done.2 = bf16[1024,192]{0,1:T(8,128)(2,1)} collective-permute-done((bf16[1024,192]{0,1:T(8,128)(2,1)}, bf16[1024,192]{0,1:T(8,128)(2,1)}, u32[]{:S(2)}, u32[]{:S(2)}) %collective-permute-start.2) | collective-permute-done | bytes 393248 | tf_op jit(solution)/shard_map/ppermute | solution.py:155
  97.8 1.8 constant_dynamic-update-slice_fusion.7
  99.7 1.8 constant_dynamic-update-slice_fusion.6
  101.5 1.8 constant_dynamic-update-slice_fusion.5
  103.2 1.8 constant_dynamic-update-slice_fusion.4
  105.0 1.8 constant_dynamic-update-slice_fusion.3
  106.8 1.8 constant_dynamic-update-slice_fusion.2
  110.2 3.8 fusion.97
  117.4 4.8 %fusion.98 = f32[1024,768]{1,0:T(8,128)} fusion(bf16[1024,768]{0,1:T(8,128)(2,1)} %add_convert_fusion, bf16[768,768]{1,0:T(8,128)(2,1)} %all-gather.15.cloned.1.call-done), kind=kOutput, calls=%fused_computation.178 | convolution fusion | flops 1207959552 | bytes 5898240 | tf_op jit(solution)/shard_map/dot_general | solution.py:23
  122.2 4.5 all-gather.17.cloned.1.call-done
  126.7 38.5 %all-gather.23.cloned.1.call-done = bf16[1,1024,768]{2,1,0:T(8,128)(2,1)} async-done(((bf16[1,256,768]{2,1,0:T(8,128)(2,1)}), bf16[1,1024,768]{2,1,0:T(8,128)(2,1)}) %all-gather.23.cloned.1.call-update) | async-done | bytes 1572880 | tf_op jit(solution)/shard_map/all_gather | solution.py:35
  165.2 5.6 %fusion.16 = bf16[1024,768]{1,0:T(8,128)(2,1)S(1)} fusion(f32[1024,768]{1,0:T(8,128)} %fusion.98, bf16[768,768]{1,0:T(8,128)(2,1)} %all-gather.17.cloned.1.call-done, bf16[1,1024,768]{2,1,0:T(8,128)(2,1)} %all-gather.23.cloned.1.call-done), kind=kOutput, calls=%fused_computation.26 | convolution fusion | flops 1223688192 | bytes 7471104 | tf_op jit(solution)/shard_map/dot_general | solution.py:31
  172.0 2.6 convolution_convert_fusion.1
  174.7 3.5 convolution_convert_fusion.3
  178.1 1.7 fusion.33
  181.4 4.3 copy.156
  186.0 1.9 copy.130
  189.8 19.1 %reduce-scatter.12.cloned.1.call-done = bf16[256,768]{0,1:T(8,128)(2,1)} async-done(((bf16[1024,768]{0,1:T(8,128)(2,1)}), bf16[256,768]{0,1:T(8,128)(2,1)}) %reduce-scatter.12.cloned.1.call-update) | async-done | bytes 393232 | tf_op jit(solution)/shard_map/reduce_scatter | solution.py:39
  208.9 2.2 multiply_reduce_fusion.3
  211.1 2.3 fusion.73
  214.1 2.4 fusion.76
  218.6 35.1 %reduce-scatter.18.cloned.1.call-done = bf16[96,1536]{1,0:T(8,128)(2,1)} async-done(((bf16[768,1536]{1,0:T(8,128)(2,1)}), bf16[96,1536]{1,0:T(8,128)(2,1)}) %reduce-scatter.18.cloned.1.call-update) | async-done | bytes 294928 | tf_op jit(solution)/shard_map/reduce_scatter | solution.py:191
  253.8 39.9 %all-gather.19.cloned.1.call-done = bf16[1024,768]{0,1:T(8,128)(2,1)} async-done(((bf16[256,768]{0,1:T(8,128)(2,1)}), bf16[1024,768]{0,1:T(8,128)(2,1)}) %all-gather.19.cloned.1.call-update) | async-done | bytes 1572880 | tf_op jit(solution)/shard_map/all_gather | solution.py:35
  293.7 2.0 convolution_convert_fusion.6
  299.2 1.9 multiply_reduce_fusion
  304.1 2.2 fusion.51
  312.0 2.5 convolution_convert_fusion
  314.9 5.0 %convolution_convert_fusion.2 = bf16[1024,768]{0,1:T(8,128)(2,1)} fusion(bf16[768,768]{1,0:T(8,128)(2,1)} %all-gather.17.cloned.1.call-done, f32[1024,768]{1,0:T(8,128)} %fusion.98), kind=kOutput, calls=%fused_computation.50 | convolution fusion | flops 1215823872 | bytes 5898240 | tf_op jit(solution)/shard_map/dot_general | solution.py:23
  321.8 2.2 all-gather.25.cloned.1.call-done
  324.0 2.4 fusion.91
  326.4 1.9 reshape.285
  328.4 2.2 copy.143
  330.5 3.6 reshape.282
  335.3 28.1 %reduce-scatter.16.cloned.1.call-done = bf16[96,768]{1,0:T(8,128)(2,1)} async-done(((bf16[768,768]{1,0:T(8,128)(2,1)}), bf16[96,768]{1,0:T(8,128)(2,1)}) %reduce-scatter.16.cloned.1.call-update) | async-done | bytes 147472 | tf_op jit(solution)/shard_map/reduce_scatter | solution.py:192
  363.4 22.1 %all-gather.2 = bf16[384,768]{1,0:T(8,128)(2,1)S(1)} all-gather(bf16[96,768]{1,0:T(8,128)(2,1)} %reduce-scatter.16.cloned.1.call-done), channel_id=4, replica_groups=mesh['seq'=4,'dp'=8] {'seq'}, dimensions={0}, use_global_device_ids=true | all-gather | bytes 737280 | tf_op jit(solution)/shard_map/all_gather | solution.py:194
  389.0 2.9 reshape.280
  391.9 13.7 %reduce-scatter.14.cloned.1.call-done = bf16[256,768]{0,1:T(8,128)(2,1)} async-done(((bf16[1024,768]{0,1:T(8,128)(2,1)}), bf16[256,768]{0,1:T(8,128)(2,1)}) %reduce-scatter.14.cloned.1.call-update) | async-done | bytes 393232 | tf_op jit(solution)/shard_map/reduce_scatter | solution.py:39
  408.7 41.2 %psum.7 = f32[4,768]{1,0:T(4,128)S(1)} all-reduce(f32[4,768]{1,0:T(4,128)S(1)} %pad_maximum_fusion.6), channel_id=1, replica_groups=mesh['seq'=4,'dp'=8] {'seq','dp'}, use_global_device_ids=true, to_apply=%region_27.28 | all-reduce | flops 3072 | bytes 24576 | tf_op jit(solution)/shard_map/psum | solution.py:214
  450.5 2.0 fusion.79
  (241 shorter events, 57.1 us)
Async XLA Ops:
  7.2 7.4 %copy-start = (bf16[384,768]{1,0:T(8,128)(2,1)S(1)}, bf16[384,768]{1,0:T(8,128)(2,1)}, u32[]{:S(2)}) copy-start(bf16[384,768]{1,0:T(8,128)(2,1)} %param.14) | copy-start | bytes 1769476
  7.2 8.2 %copy-start.57 = (bf16[96]{0:T(256)(128)(2,1)S(1)}, bf16[96]{0:T(256)(128)(2,1)}, u32[]{:S(2)}) copy-start(bf16[96]{0:T(256)(128)(2,1)} %param.18) | copy-start | bytes 580
  7.2 8.2 %copy-start.58 = (bf16[96]{0:T(256)(128)(2,1)S(1)}, bf16[96]{0:T(256)(128)(2,1)}, u32[]{:S(2)}) copy-start(bf16[96]{0:T(256)(128)(2,1)} %param.17) | copy-start | bytes 580
  7.2 8.2 %copy-start.59 = (bf16[96]{0:T(256)(128)(2,1)S(1)}, bf16[96]{0:T(256)(128)(2,1)}, u32[]{:S(2)}) copy-start(bf16[96]{0:T(256)(128)(2,1)} %param.16) | copy-start | bytes 580
  7.2 8.2 %copy-start.60 = (bf16[96]{0:T(256)(128)(2,1)S(1)}, bf16[96]{0:T(256)(128)(2,1)}, u32[]{:S(2)}) copy-start(bf16[96]{0:T(256)(128)(2,1)} %param.15) | copy-start | bytes 580
  7.2 21.3 %copy-start.29 = (bf16[96,2304]{1,0:T(8,128)(2,1)S(1)}, bf16[96,2304]{1,0:T(8,128)(2,1)}, u32[]{:S(2)}) copy-start(bf16[96,2304]{1,0:T(8,128)(2,1)} %param.11) | copy-start | bytes 1327108
  7.2 43.4 %all-gather.21.cloned.1.call-start = ((), (), s32[]{:S(2)}) async-start(), calls=%async_computation.12 | async-start | bytes 1966080 | tf_op jit(solution)/shard_map/all_gather | solution.py:35
  9.3 100.9 %all-gather.13.cloned.1.call-start = ((), (), s32[]{:S(2)}) async-start(), calls=%async_computation.5 | async-start | bytes 1327104 | tf_op jit(solution)/shard_map/all_gather | solution.py:142
  10.1 107.3 %all-gather.15.cloned.1.call-start = ((), (), s32[]{:S(2)}) async-start(), calls=%async_computation.6 | async-start | bytes 1327104 | tf_op jit(solution)/shard_map/all_gather | solution.py:143
  14.5 112.2 %all-gather.17.cloned.1.call-start = ((), (), s32[]{:S(2)}) async-start(), calls=%async_computation.7 | async-start | bytes 1327104 | tf_op jit(solution)/shard_map/all_gather | solution.py:144
  15.3 149.9 %all-gather.23.cloned.1.call-start = ((), (), s32[]{:S(2)}) async-start(), calls=%async_computation.13 | async-start | bytes 1966080 | tf_op jit(solution)/shard_map/all_gather | solution.py:35
  26.5 27.9 %copy-start.53 = (f32[768]{0:T(1024)}, f32[768]{0:T(1024)S(1)}, u32[]{:S(2)}) copy-start(f32[768]{0:T(1024)S(1)} %get-tuple-element.82) | copy-start | bytes 9220
  41.4 14.3 %copy-start.25 = (bf16[768,576]{1,0:T(8,128)(2,1)}, bf16[768,576]{1,0:T(8,128)(2,1)S(1)}, u32[]{:S(2)}) copy-start(bf16[768,576]{1,0:T(8,128)(2,1)S(1)} %all_gather.38) | copy-start | bytes 2654212
  50.7 3.7 copy-start.5
  55.9 6.0 %copy-start.20 = (bf16[1024,192]{0,1:T(8,128)(2,1)}, bf16[1024,192]{0,1:T(8,128)(2,1)S(1)}, u32[]{:S(2)}) copy-start(bf16[1024,192]{0,1:T(8,128)(2,1)S(1)} %get-tuple-element.93) | copy-start | bytes 1179652
  58.6 6.2 %copy-start.12 = (bf16[3,64,512]{2,1,0:T(8,128)(2,1)}, bf16[3,64,512]{2,1,0:T(8,128)(2,1)S(1)}, u32[]{:S(2)}) copy-start(bf16[3,64,512]{2,1,0:T(8,128)(2,1)S(1)} %fusion.60) | copy-start | bytes 589828
  65.4 11.3 %collective-permute-start = (bf16[1024,192]{0,1:T(8,128)(2,1)S(1)}, bf16[1024,192]{0,1:T(8,128)(2,1)S(1)}, u32[]{:S(2)}, u32[]{:S(2)}) collective-permute-start(bf16[1024,192]{0,1:T(8,128)(2,1)S(1)} %pad_maximum_fusion.3), channel_id=1, source_target_pairs={{0,8},{8,16},{16,24},{24,0},{1,9},{9,17},{17,25},{25,1},{2,10},{10... | collective-permute-start | bytes 1179656 | tf_op jit(solution)/shard_map/ppermute | solution.py:155
  77.5 10.5 %collective-permute-start.1 = (bf16[1024,192]{0,1:T(8,128)(2,1)S(1)}, bf16[1024,192]{0,1:T(8,128)(2,1)}, u32[]{:S(2)}, u32[]{:S(2)}) collective-permute-start(bf16[1024,192]{0,1:T(8,128)(2,1)S(1)} %collective-permute-done), channel_id=1, source_target_pairs={{0,8},{8,16},{16,24},{24,0},{1,9},{9,17},{17,25},{25,1},{2,10},{10... | collective-permute-start | bytes 1179656 | tf_op jit(solution)/shard_map/ppermute | solution.py:155
  88.0 9.9 %collective-permute-start.2 = (bf16[1024,192]{0,1:T(8,128)(2,1)}, bf16[1024,192]{0,1:T(8,128)(2,1)}, u32[]{:S(2)}, u32[]{:S(2)}) collective-permute-start(bf16[1024,192]{0,1:T(8,128)(2,1)} %collective-permute-done.1), channel_id=1, source_target_pairs={{0,8},{8,16},{16,24},{24,0},{1,9},{9,17},{17,25},{25,1},{2,10},{10... | collective-permute-start | bytes 1179656 | tf_op jit(solution)/shard_map/ppermute | solution.py:155
  88.0 120.9 %reduce-scatter.12.cloned.1.call-start = ((), (), s32[]{:S(2)}) async-start(), calls=%async_computation.9 | async-start | bytes 1966080 | tf_op jit(solution)/shard_map/reduce_scatter | solution.py:39
  88.2 20.4 %copy-start.23 = (bf16[1024,192]{0,1:T(8,128)(2,1)S(1)}, bf16[1024,192]{0,1:T(8,128)(2,1)}, u32[]{:S(2)}) copy-start(bf16[1024,192]{0,1:T(8,128)(2,1)} %copy-done.22) | copy-start | bytes 1179652
  88.2 21.1 %copy-start.13 = (bf16[3,64,512]{2,1,0:T(8,128)(2,1)S(1)}, bf16[3,64,512]{2,1,0:T(8,128)(2,1)}, u32[]{:S(2)}) copy-start(bf16[3,64,512]{2,1,0:T(8,128)(2,1)} %copy-done.12) | copy-start | bytes 589828
  88.3 21.1 %copy-start.15 = (bf16[3,64,512]{2,1,0:T(8,128)(2,1)S(1)}, bf16[3,64,512]{2,1,0:T(8,128)(2,1)}, u32[]{:S(2)}) copy-start(bf16[3,64,512]{2,1,0:T(8,128)(2,1)} %copy-done.14) | copy-start | bytes 589828
  165.2 6.7 %copy-start.62 = (bf16[768,768]{1,0:T(8,128)(2,1)S(1)}, bf16[768,768]{1,0:T(8,128)(2,1)}, u32[]{:S(2)}) copy-start(bf16[768,768]{1,0:T(8,128)(2,1)} %all-gather.15.cloned.1.call-done) | copy-start | bytes 3538948
  174.6 79.1 %reduce-scatter.18.cloned.1.call-start = ((), (), s32[]{:S(2)}) async-start(), calls=%async_computation.16 | async-start | bytes 2654208 | tf_op jit(solution)/shard_map/reduce_scatter | solution.py:191
  174.6 3.5 copy-start.61
  174.6 3.5 copy-start.63
  185.7 107.9 %all-gather.19.cloned.1.call-start = ((), (), s32[]{:S(2)}) async-start(), calls=%async_computation.10 | async-start | bytes 1966080 | tf_op jit(solution)/shard_map/all_gather | solution.py:35
  216.5 107.5 %all-gather.25.cloned.1.call-start = ((), (), s32[]{:S(2)}) async-start(), calls=%async_computation.14 | async-start | bytes 1474560 | tf_op jit(solution)/shard_map/all_gather | solution.py:193
  253.7 109.6 %reduce-scatter.16.cloned.1.call-start = ((), (), s32[]{:S(2)}) async-start(), calls=%async_computation.15 | async-start | bytes 1327104 | tf_op jit(solution)/shard_map/reduce_scatter | solution.py:192
  302.5 3.8 copy-start.10
  303.7 5.2 %copy-start.30 = (bf16[3,64,512]{2,1,0:T(8,128)(2,1)}, bf16[3,64,512]{2,1,0:T(8,128)(2,1)S(1)}, u32[]{:S(2)}) copy-start(bf16[3,64,512]{2,1,0:T(8,128)(2,1)S(1)} %fusion.59) | copy-start | bytes 589828
  304.1 4.8 %copy-start.32 = (bf16[3,64,512]{2,1,0:T(8,128)(2,1)}, bf16[3,64,512]{2,1,0:T(8,128)(2,1)S(1)}, u32[]{:S(2)}) copy-start(bf16[3,64,512]{2,1,0:T(8,128)(2,1)S(1)} %fusion.58) | copy-start | bytes 589828
  311.9 93.8 %reduce-scatter.14.cloned.1.call-start = ((), (), s32[]{:S(2)}) async-start(), calls=%async_computation.11 | async-start | bytes 1966080 | tf_op jit(solution)/shard_map/reduce_scatter | solution.py:39
  314.5 5.4 %copy-start.4 = (bf16[1,256,768]{1,2,0:T(8,128)(2,1)S(1)}, bf16[1,256,768]{1,2,0:T(8,128)(2,1)}, u32[]{:S(2)}) copy-start(bf16[1,256,768]{1,2,0:T(8,128)(2,1)} %copy.123) | copy-start | bytes 1179652
  314.5 6.1 %copy-start.40 = (f32[768]{0:T(1024)S(1)}, f32[768]{0:T(1024)}, u32[]{:S(2)}) copy-start(f32[768]{0:T(1024)} %get-tuple-element.79) | copy-start | bytes 9220
  314.5 6.7 %copy-start.41 = (f32[768]{0:T(1024)S(1)}, f32[768]{0:T(1024)}, u32[]{:S(2)}) copy-start(f32[768]{0:T(1024)} %get-tuple-element.70) | copy-start | bytes 9220
  314.6 135.9 %reduce-scatter.10.cloned.1.call-start = ((), (), s32[]{:S(2)}) async-start(), calls=%async_computation.8 | async-start | bytes 1966080 | tf_op jit(solution)/shard_map/reduce_scatter | solution.py:39
  387.3 18.3 %copy-start.44 = (f32[256]{0:T(256)S(1)}, f32[256]{0:T(256)}, u32[]{:S(2)}) copy-start(f32[256]{0:T(256)} %broadcast_multiply_fusion.2) | copy-start | bytes 3076
  387.3 21.3 %copy-start.49 = (f32[1,768]{1,0:T(1,128)S(1)}, f32[1,768]{1,0:T(1,128)}, u32[]{:S(2)}) copy-start(f32[1,768]{1,0:T(1,128)} %reshape.279) | copy-start | bytes 9220
  387.3 21.3 %copy-start.50 = (f32[1,768]{1,0:T(1,128)S(1)}, f32[1,768]{1,0:T(1,128)}, u32[]{:S(2)}) copy-start(f32[1,768]{1,0:T(1,128)} %reshape.278) | copy-start | bytes 9220
  387.3 63.1 %copy-start.7 = (bf16[256,768]{0,1:T(8,128)(2,1)S(1)}, bf16[256,768]{0,1:T(8,128)(2,1)}, u32[]{:S(2)}) copy-start(bf16[256,768]{0,1:T(8,128)(2,1)} %reduce-scatter.12.cloned.1.call-done) | copy-start | bytes 1179652
  387.4 63.1 %copy-start.8 = (bf16[1,256,768]{1,2,0:T(8,128)(2,1)S(1)}, bf16[1,256,768]{1,2,0:T(8,128)(2,1)}, u32[]{:S(2)}) copy-start(bf16[1,256,768]{1,2,0:T(8,128)(2,1)} %copy.130) | copy-start | bytes 1179652
  387.4 63.1 %copy-start.38 = (f32[256]{0:T(256)S(1)}, f32[256]{0:T(256)}, u32[]{:S(2)}) copy-start(f32[256]{0:T(256)} %broadcast_multiply_fusion.3) | copy-start | bytes 3076
  387.4 63.1 %copy-start.46 = (f32[256]{0:T(256)S(1)}, f32[256]{0:T(256)}, u32[]{:S(2)}) copy-start(f32[256]{0:T(256)} %copy-done.45) | copy-start | bytes 3076
  387.4 63.1 %copy-start.48 = (f32[256]{0:T(256)S(1)}, f32[256]{0:T(256)}, u32[]{:S(2)}) copy-start(f32[256]{0:T(256)} %copy-done.47) | copy-start | bytes 3076
  387.4 63.1 %copy-start.52 = (f32[256]{0:T(256)S(1)}, f32[256]{0:T(256)}, u32[]{:S(2)}) copy-start(f32[256]{0:T(256)} %copy-done.51) | copy-start | bytes 3076
  405.6 48.7 %copy-start.1 = (bf16[384,768]{1,0:T(8,128)(2,1)S(1)}, bf16[384,768]{1,0:T(8,128)(2,1)}, u32[]{:S(2)}) copy-start(bf16[384,768]{1,0:T(8,128)(2,1)} %param.14) | copy-start | bytes 1769476
  (34 other events, 58.9 us)
Sparse Core Ops, SparseCore 0:
  10.2 40.3 all-gather.20
  52.5 22.2 all-gather.12
  76.8 24.0 all-gather.14
  102.6 24.0 all-gather.16
  128.1 37.0 all-gather.22
  174.7 34.1 reduce-scatter.11
  212.3 41.4 reduce-scatter.17
  255.9 37.6 all-gather.18
  295.3 28.6 all-gather.24
  327.5 35.8 reduce-scatter.15
  365.7 39.8 reduce-scatter.13
  407.8 35.1 reduce-scatter.9
